TPU v7x, 128 devices: a whole 4x4x4 slice. The times are simulated.
128 devices in a mesh: dp: 16 (over y_hi, x, core), tensor: 4 (over z), proj: 2 (over y_lo).
Axes of the slice: x: 4, y: 4 (y_hi: 2, y_lo: 2; y = y_hi * 2 + y_lo), z: 4, core: 2. Of those that a mesh axis runs over, the one named last changes fastest.
Arguments:
- acts: bfloat16 [160, 1024, 4096], P(('dp', 'proj'), None, 'tensor'), may hold values from -6 to 6
- cotangent: bfloat16 [160, 1024, 4096], P(('dp', 'proj'), None, 'tensor'), may hold values from -6 to 6
- adapter_down: bfloat16 [4096, 128], P('tensor'), may hold values from -0.09375 to 0.09375
- adapter_up: bfloat16 [128, 4096], P(None, 'tensor'), may hold values from -0.09375 to 0.09375
- lengths: int32 [160], P(('dp', 'proj')), may hold values from 256 to 1024, as said below
- projection_rows: int32 [4, 32, 64], P('tensor', ('dp', 'proj')), may hold values from 0 to 31
- projection_blocks: bfloat16 [4, 32, 64, 256, 128], P('tensor', ('dp', 'proj')), may hold values from -1 to 1
Outputs:
- features: float32 [160, 8192], P(('dp', 'proj'), 'tensor')
Inputs may be any that keep to these rules, and one draw needn't show every extreme that they name: `lengths`: every sequence has at least 256 tokens; some sequence has exactly 1024.
All inputs are finite; a program needn't handle non-finite values.
Results may differ from a plain program's by a relative error of at most 0.0041.
Values may be sent and summed in bfloat16 or wider, within the bound.
A program may use at most 128 MiB of HBM per device.

v0:
```python
import jax
import jax.numpy as jnp
from jax import lax
from jax.sharding import PartitionSpec as P


def local(acts, cotangent, adapter_down, adapter_up, lengths, projection_rows, projection_blocks):
    sequence_per_device, length, rows_of_width = acts.shape
    adapter_rank = adapter_down.shape[1]
    reduced_hidden = jnp.einsum(
        "spu,un->spn", acts, adapter_down, preferred_element_type=jnp.float32
    )
    reduced_upstream = jnp.einsum(
        "iuq,xq->iux", cotangent, adapter_up, preferred_element_type=jnp.float32
    )
    positions = jnp.arange(length, dtype=jnp.int32)
    token_weight = (positions[None, :] < lengths[:, None]).astype(jnp.float32) / lengths[
        :, None
    ].astype(jnp.float32)
    h_total, u_total = lax.psum((reduced_hidden, reduced_upstream), "tensor")
    hidden_w = (h_total * token_weight[:, :, None]).astype(jnp.bfloat16)
    upper_w = (u_total * token_weight[:, :, None]).astype(jnp.bfloat16)
    grad_a = jnp.einsum("etd,etr->edr", acts, upper_w, preferred_element_type=jnp.float32)
    grad_b = jnp.einsum("etd,etr->edr", cotangent, hidden_w, preferred_element_type=jnp.float32)
    gradient_list = jnp.concatenate([grad_a, grad_b], axis=2).astype(jnp.bfloat16)
    rows_per_range = rows_of_width // (lax.axis_size("dp") * lax.axis_size("proj"))
    direct_gradient = gradient_list.reshape(1, sequence_per_device, rows_of_width, 2 * adapter_rank)
    landed_blocks = lax.all_to_all(
        direct_gradient, ("dp", "proj"), split_axis=2, concat_axis=0, tiled=True
    )
    incoming_blocks = landed_blocks.reshape(-1, rows_per_range, 2 * adapter_rank)
    output_block_count = projection_blocks.shape[2]
    output_block = projection_blocks.shape[4]
    row_pick = projection_rows.reshape(output_block_count)
    block_list = projection_blocks.reshape(output_block_count, 2 * adapter_rank, output_block)
    chosen = jnp.take(incoming_blocks, row_pick, axis=1)
    contrib = jnp.einsum("eok,okc->eoc", chosen, block_list, preferred_element_type=jnp.float32)
    own_rows = lax.psum_scatter(
        contrib.reshape(incoming_blocks.shape[0], output_block_count * output_block),
        ("dp", "proj"),
        scatter_dimension=0,
        tiled=True,
    )
    result = lax.psum_scatter(own_rows, "tensor", scatter_dimension=1, tiled=True)
    return result


def solution(mesh):
    placed = (
        P(("dp", "proj"), None, "tensor"),
        P(("dp", "proj"), None, "tensor"),
        P("tensor", None),
        P(None, "tensor"),
        P(("dp", "proj")),
        P("tensor", ("dp", "proj"), None),
        P("tensor", ("dp", "proj"), None, None, None),
    )
    return jax.shard_map(
        local, mesh=mesh, in_specs=placed, out_specs=P(("dp", "proj"), "tensor"), check_vma=False
    )
```

profile of v0, /device:TPU:1, one launch (start us, length us, event | category | flops | bytes accessed | tf_op | source)
XLA Modules:
  0.0 368.6 jit_solution(486154336639419122)
XLA Ops:
  6.5 0.9 copy-done
  7.5 8.5 %fusion.15 = f32[5,1024,128]{2,1,0:T(8,128)} fusion(bf16[5,1024,1024]{2,1,0:T(8,128)(2,1)} %param.7, bf16[1024,128]{1,0:T(8,128)(2,1)S(1)} %copy-done), kind=kOutput, calls=%fused_computation.18 | convolution fusion | flops 1342177280 | bytes 13369344 | tf_op jit(solution)/shard_map/spu,un->spn/dot_general | solution.py:10
  16.0 4.5 %fusion.17 = f32[5,1024,128]{2,1,0:T(8,128)} fusion(bf16[5,1024,1024]{2,1,0:T(8,128)(2,1)S(1)} %copy-done.2, bf16[128,1024]{1,0:T(8,128)(2,1)S(1)} %copy-done.4), kind=kOutput, calls=%fused_computation.20 | convolution fusion | flops 1342177280 | bytes 13369344 | tf_op jit(solution)/shard_map/iuq,xq->iux/dot_general | solution.py:13
  20.5 0.6 copy-done.5
  21.2 112.9 %all-reduce.7.cloned.1.call-done = (f32[5,1024,128]{2,1,0:T(8,128)}, f32[5,1024,128]{2,1,0:T(8,128)}) async-done(((f32[5,1024,128]{2,1,0:T(8,128)}, f32[5,1024,128]{2,1,0:T(8,128)}), (f32[5,1024,128]{2,1,0:T(8,128)}, f32[5,1024,128]{2,1,0:T(8,128)})) %all-reduce.7.cloned.1.call-update) | async-done | bytes 5242896 | tf_op jit(solution)/shard_map/psum | solution.py:20
  134.1 7.2 %fusion.11 = bf16[1,5,1024,128]{2,3,1,0:T(8,128)(2,1)S(1)} fusion(bf16[5,1024,1024]{2,1,0:T(8,128)(2,1)} %param.7, f32[5,1024,128]{2,1,0:T(8,128)} %get-tuple-element.6, f32[5,1024]{1,0:T(8,128)S(1)} %convert_divide_fusion), kind=kOutput, calls=%fused_computation.14 | convolution fusion | flops 1344143360 | bytes 14438400 | tf_op jit(solution)/shard_map/etd,etr->edr/dot_general | solution.py:23
  141.4 0.7 copy-done.3
  142.1 2.4 fusion.12
  144.5 0.2 pad_maximum_fusion
  144.7 4.9 %copy.14 = bf16[1,5,1024,256]{3,1,0,2:T(8,128)(2,1)} copy(bf16[1,5,1024,256]{2,3,1,0:T(8,128)(2,1)S(1)} %pad_maximum_fusion) | data formatting | bytes 5242880 | tf_op jit(solution)/shard_map/concatenate | solution.py:25
  149.6 7.8 %all-to-all-start = ((bf16[1,5,1024,256]{3,1,0,2:T(8,128)(2,1)}), bf16[1,5,1024,256]{3,1,0,2:T(8,128)(2,1)}, u32[]{:S(2)}, u32[]{:S(2)}) async-start(bf16[1,5,1024,256]{3,1,0,2:T(8,128)(2,1)} %copy.14), calls=%async_computation | async-start | bytes 8388608 | tf_op jit(solution)/shard_map/all_to_all | solution.py:28
  157.4 0.2 all-reduce.5.cloned.1.call-start
  157.7 54.3 %all-to-all-done = bf16[1,5,1024,256]{3,1,0,2:T(8,128)(2,1)} async-done(((bf16[1,5,1024,256]{3,1,0,2:T(8,128)(2,1)}), bf16[1,5,1024,256]{3,1,0,2:T(8,128)(2,1)}, u32[]{:S(2)}, u32[]{:S(2)}) %all-to-all-start) | async-done | bytes 2621472 | tf_op jit(solution)/shard_map/all_to_all | solution.py:28
  212.0 2.8 copy.15
  214.8 0.2 copy.16
  215.0 1.5 copy.17
  216.5 3.2 gather_fusion
  219.7 5.3 %fusion.6 = f32[64,20,8,128]{3,2,1,0:T(8,128)S(1)} fusion(bf16[1,1,64,256,128]{4,3,2,1,0:T(8,128)(2,1)} %param.13, bf16[64,160,256]{2,1,0:T(8,128)(2,1)} %gather_fusion, pred[64]{0:T(512)(128)(4,1)S(1)} %compare_and_fusion), kind=kOutput, calls=%fused_computation.11 | convolution fusion | flops 673710080 | bytes 14680128 | tf_op jit(solution)/shard_map/eok,okc->eoc/dot_general | solution.py:37
  225.1 2.9 copy.23
  228.1 0.6 copy-done.7
  228.6 0.6 dynamic-slice
  229.9 111.4 %all-reduce.5.cloned.1.call-done = f32[160,8192]{1,0:T(8,128)} async-done(((f32[160,8192]{1,0:T(8,128)}), f32[160,8192]{1,0:T(8,128)}) %all-reduce.5.cloned.1.call-update) | async-done | bytes 5242896
  341.3 1.8 constant_dynamic-slice_fusion
  343.1 19.0 %reduce-scatter.2.cloned.1.call-done = f32[5,2048]{1,0:T(8,128)} async-done(((f32[5,8192]{1,0:T(8,128)}), f32[5,2048]{1,0:T(8,128)}) %reduce-scatter.2.cloned.1.call-update) | async-done | bytes 40976 | tf_op jit(solution)/shard_map/reduce_scatter | solution.py:44
  (29 shorter events, 0.2 us)
Async XLA Ops:
  6.5 1.0 copy-start
  6.5 9.4 %copy-start.4 = (bf16[128,1024]{1,0:T(8,128)(2,1)S(1)}, bf16[128,1024]{1,0:T(8,128)(2,1)}, u32[]{:S(2)}) copy-start(bf16[128,1024]{1,0:T(8,128)(2,1)} %param.10) | copy-start | bytes 786436
  6.5 127.6 %all-reduce.7.cloned.1.call-start = ((), (), s32[]{:S(2)}) async-start(), calls=%async_computation.4 | async-start | bytes 10485760 | tf_op jit(solution)/shard_map/psum | solution.py:20
  7.5 8.5 %copy-start.2 = (bf16[5,1024,1024]{2,1,0:T(8,128)(2,1)S(1)}, bf16[5,1024,1024]{2,1,0:T(8,128)(2,1)}, u32[]{:S(2)}) copy-start(bf16[5,1024,1024]{2,1,0:T(8,128)(2,1)} %param.8) | copy-start | bytes 31457284
  20.5 0.7 copy-start.5
  20.5 120.9 %slice-start = ((s8[10485760]{0:T(1024)(128)(4,1)}), s8[2097152]{0:T(1024)(128)(4,1)S(1)}, s32[]{:S(2)}) async-start(s8[10485760]{0:T(1024)(128)(4,1)} %bitcast.45), calls=%async_computation.5 | async-start | bytes 4194304
  134.1 7.3 %slice-start.1 = ((s8[10485760]{0:T(1024)(128)(4,1)}), s8[4194304]{0:T(1024)(128)(4,1)S(1)}, s32[]{:S(2)}) async-start(s8[10485760]{0:T(1024)(128)(4,1)} %bitcast.45), calls=%async_computation.6 | async-start | bytes 8388608
  134.1 7.3 %slice-start.2 = ((s8[10485760]{0:T(1024)(128)(4,1)}), s8[4194304]{0:T(1024)(128)(4,1)S(1)}, s32[]{:S(2)}) async-start(s8[10485760]{0:T(1024)(128)(4,1)} %bitcast.45), calls=%async_computation.7 | async-start | bytes 8388608
  134.1 8.0 %copy-start.3 = (f32[5,1024,128]{2,1,0:T(8,128)S(1)}, f32[5,1024,128]{2,1,0:T(8,128)}, u32[]{:S(2)}) copy-start(f32[5,1024,128]{2,1,0:T(8,128)} %get-tuple-element.5) | copy-start | bytes 7864324
  149.6 8.0 %copy-start.6 = (s32[1,1,64]{2,1,0:T(1,128)S(1)}, s32[1,1,64]{2,1,0:T(1,128)}, u32[]{:S(2)}) copy-start(s32[1,1,64]{2,1,0:T(1,128)} %param.12) | copy-start | bytes 772
  149.6 62.3 %all-to-all-start = ((bf16[1,5,1024,256]{3,1,0,2:T(8,128)(2,1)}), bf16[1,5,1024,256]{3,1,0,2:T(8,128)(2,1)}, u32[]{:S(2)}, u32[]{:S(2)}) async-start(bf16[1,5,1024,256]{3,1,0,2:T(8,128)(2,1)} %copy.14), calls=%async_computation | async-start | bytes 8388608 | tf_op jit(solution)/shard_map/all_to_all | solution.py:28
  157.4 183.9 %all-reduce.5.cloned.1.call-start = ((), (), s32[]{:S(2)}) async-start(), calls=%async_computation.3 | async-start | bytes 10485760
  225.0 137.1 %copy-start.1 = (bf16[1024,128]{1,0:T(8,128)(2,1)S(1)}, bf16[1024,128]{1,0:T(8,128)(2,1)}, u32[]{:S(2)}) copy-start(bf16[1024,128]{1,0:T(8,128)(2,1)} %param.9) | copy-start | bytes 786436
  228.0 0.7 copy-start.7
  228.0 134.1 %reduce-scatter.2.cloned.1.call-start = ((), (), s32[]{:S(2)}) async-start(), calls=%async_computation.2 | async-start | bytes 327680 | tf_op jit(solution)/shard_map/reduce_scatter | solution.py:44
Sparse Core Ops, SparseCore 0:
  20.6 113.4 all-reduce.6
  228.1 113.1 all-reduce.4
  343.8 18.2 reduce-scatter.1
where the time goes:
time: 370 us; the launch traced here: 369 us
  waiting for transfers between devices  298 us (81%)
  matrix products  27.9 us (8%)
  local copies, waits for them, and re-layouts  20.8 us (6%)
  between operations  13.9 us (4%)
  starting transfers between devices  8.02 us (2%)
    psum x1, waiting for transfers between devices, local(): h_total, u_total = lax.psum((reduced_hidden, reduced_upstream), 'tensor')  113 us
    unnamed x4, waiting for transfers between devices  111 us
    all_to_all x1, waiting for transfers between devices, local(): lax.all_to_all(direct_gradient, ('dp', 'proj'), split_axis=2, concat_axis...  54.3 us
    reduce_scatter x1, waiting for transfers between devices, local(): lax.psum_scatter(own_rows, 'tensor', scatter_dimension=1, tiled=True)  19 us
    dot_general x1, matrix products, local(): jnp.einsum('spu,un->spn', acts, adapter_down, preferred_element_type=jnp....  8.5 us
    all_to_all x1, starting transfers between devices, local(): lax.all_to_all(direct_gradient, ('dp', 'proj'), split_axis=2, concat_axis...  7.76 us
  transfers between devices with their start and end apart: 4, of which 4 were waited for; matrix products, arithmetic and copies ran while one was open for 0% of the time, Pallas kernels for 0%

commit v1 on v0

v1 whole, which is shorter than its diff:
```python
import functools

import jax
import jax.numpy as jnp
from jax import lax
from jax.experimental import pallas as pl
from jax.experimental.pallas import tpu as pltpu
from jax.sharding import PartitionSpec as P

MESH = pl.DeviceIdType.MESH
F32 = jnp.float32
BF16 = jnp.bfloat16
SEQ = 5
GROUPS = 32
CHIPS = 16


def group_of(y, x, core):
    return ((y // 2 * 4 + x) * 2 + core) * 2 + y % 2


def kernel(
    acts, cot, down, up, lens, rows, blocks, out,
    a_buf, c_buf, b_buf, own, relay_f, part, relay_in, fin_in, gath, grads, land, turned,
    contrib, cross, summed, plane, fsend, frecv,
    load_sem, block_sem, rs_send, rs_recv, ag_send, ag_recv, a2a_send, a2a_recv,
    cross_sem, plane_send, plane_recv, fin_send, fin_recv,
):
    dp, pj, me = lax.axis_index("dp"), lax.axis_index("proj"), lax.axis_index("tensor")
    group = dp * 2 + pj
    core = dp % 2
    xx = (dp // 2) % 4
    yy = (dp // 8) * 2 + pj
    chip = (dp // 2) * 2 + pj
    right, left, far = (me + 1) % 4, (me + 3) % 4, (me + 2) % 4

    def at(g, z):
        return {"dp": g // 2, "proj": g % 2, "tensor": z}

    def peer(k):
        return group_of((yy + k // 8) % 4, (xx + (k // 2) % 4) % 4, (core + k % 2) % 2)

    def back(k):
        return group_of((yy + 4 - k // 8) % 4, (xx + 4 - (k // 2) % 4) % 4, (core + k % 2) % 2)

    def loads(e):
        return (
            pltpu.make_async_copy(acts.at[e], a_buf.at[e], load_sem.at[0, e]),
            pltpu.make_async_copy(cot.at[e], c_buf.at[e], load_sem.at[1, e]),
        )

    for e in range(SEQ):
        for copy in loads(e):
            copy.start()
    block_load = pltpu.make_async_copy(blocks, b_buf, block_sem)
    block_load.start()

    barrier = pltpu.get_barrier_semaphore()

    def greet(k, _):
        pl.semaphore_signal(barrier, inc=1, device_id=at(back(k), me), device_id_type=MESH)
        return 0

    lax.fori_loop(1, GROUPS, greet, 0)
    for z in (left, right):
        pl.semaphore_signal(barrier, inc=1, device_id=at(group, z), device_id_type=MESH)

    def greet_final(k, _):
        g, z = me * 8 + k // 4, k % 4

        @pl.when(jnp.logical_or(g != group, z != me))
        def _():
            pl.semaphore_signal(barrier, inc=1, device_id=at(g, z), device_id_type=MESH)

        return 0

    lax.fori_loop(0, 32, greet_final, 0)
    goal = group // 8
    pl.semaphore_wait(barrier, 31 + 2 + jnp.where(goal == me, 31, 32))

    def remote(src, dst, send, recv, g, z):
        return pltpu.make_async_remote_copy(
            src_ref=src, dst_ref=dst, send_sem=send, recv_sem=recv, device_id=at(g, z), device_id_type=MESH
        )

    def rs_copy(e, n):
        src, dst, z = (
            lambda: (part.at[e, far, 0], relay_in.at[e, 1], left),
            lambda: (part.at[e, far, 1], relay_in.at[e, 0], right),
            lambda: (part.at[e, right, 0], fin_in.at[e, 0], right),
            lambda: (part.at[e, left, 1], fin_in.at[e, 3], left),
            lambda: (part.at[e, right, 1], fin_in.at[e, 1], right),
            lambda: (part.at[e, left, 0], fin_in.at[e, 2], left),
        )[n]()
        return remote(src, dst, rs_send.at[e, n], rs_recv.at[e, n], group, z)

    def ag_copy(e, n):
        q, half, z = (
            (me, 0, right), (me, 1, left), (me, 1, right), (me, 0, left), (left, 0, right), (right, 1, left),
        )[n]
        block = gath.at[e, q * 2 + half]
        return remote(block, block, ag_send.at[e, n], ag_recv.at[e, n], group, z)

    def a2a_copy(e, k):
        g = peer(k)
        return remote(grads.at[e, g], land.at[e, group], a2a_send.at[e], a2a_recv.at[e], g, me)

    def low(e):
        for copy in loads(e):
            copy.wait()

        def partial(q):
            h = jnp.dot(a_buf[e, q], down[...], preferred_element_type=F32)
            u = lax.dot_general(c_buf[e, q], up[...], (((1,), (1,)), ((), ())), preferred_element_type=F32)
            return h, u

        h, u = partial(far)
        part[e, far, :, :, 0:128] = h.astype(BF16).reshape(2, 128, 128)
        part[e, far, :, :, 128:256] = u.astype(BF16).reshape(2, 128, 128)
        rs_copy(e, 0).start()
        rs_copy(e, 1).start()
        h, u = partial(right)
        part[e, right, 0, :, 0:128] = h[0:128].astype(BF16)
        part[e, right, 0, :, 128:256] = u[0:128].astype(BF16)
        relay_f[e, 0, :, 0:128] = h[128:256]
        relay_f[e, 0, :, 128:256] = u[128:256]
        rs_copy(e, 2).start()
        h, u = partial(left)
        part[e, left, 1, :, 0:128] = h[128:256].astype(BF16)
        part[e, left, 1, :, 128:256] = u[128:256].astype(BF16)
        relay_f[e, 1, :, 0:128] = h[0:128]
        relay_f[e, 1, :, 128:256] = u[0:128]
        rs_copy(e, 3).start()
        h, u = partial(me)
        own[e, :, 0:128] = h
        own[e, :, 128:256] = u

    def relay(e):
        rs_copy(e, 1).wait_recv()
        part[e, right, 1] = (relay_f[e, 0] + relay_in[e, 0].astype(F32)).astype(BF16)
        rs_copy(e, 4).start()
        rs_copy(e, 0).wait_recv()
        part[e, left, 0] = (relay_f[e, 1] + relay_in[e, 1].astype(F32)).astype(BF16)
        rs_copy(e, 5).start()

    def finish(e):
        length = jnp.full((128, 256), lens[e], jnp.int32)

        def half(n, first, second):
            place = lax.broadcasted_iota(jnp.int32, (128, 256), 0) + (me * 256 + n * 128)
            weight = jnp.where(place < length, 1.0 / length.astype(F32), 0.0)
            total = own[e, n * 128 : n * 128 + 128] + (fin_in[e, first].astype(F32) + fin_in[e, second].astype(F32))
            gath[e, me * 2 + n] = (total * weight).astype(BF16)

        rs_copy(e, 2).wait_recv()
        rs_copy(e, 5).wait_recv()
        half(0, 0, 2)
        ag_copy(e, 0).start()
        rs_copy(e, 3).wait_recv()
        rs_copy(e, 4).wait_recv()
        half(1, 3, 1)
        ag_copy(e, 1).start()
        ag_copy(e, 2).start()
        ag_copy(e, 3).start()

    def forward(e):
        ag_copy(e, 0).wait_recv()
        ag_copy(e, 4).start()
        ag_copy(e, 1).wait_recv()
        ag_copy(e, 5).start()

    def gradient(e):
        for n in (2, 3, 4, 5):
            ag_copy(e, n).wait_recv()
        for side in (0, 1):
            buf = (a_buf, c_buf)[side]
            other = gath[e, :, :, 128 - side * 128 : 256 - side * 128].reshape(1024, 128)

            def tile(w, _):
                wide = buf[e, :, :, pl.ds(pl.multiple_of(w * 256, 256), 256)].reshape(1024, 256)
                g = lax.dot_general(wide, other, (((0,), (0,)), ((), ())), preferred_element_type=F32)
                grads[e, pl.ds(w * 8, 8), :, side * 128 : side * 128 + 128] = g.astype(BF16).reshape(8, 32, 128)
                return 0

            lax.fori_loop(0, 4, tile, 0)

        pltpu.make_async_copy(grads.at[e, group], land.at[e, group], a2a_recv.at[e]).start()

        def send(k, _):
            a2a_copy(e, k).start()
            return 0

        lax.fori_loop(1, GROUPS, send, 0)

    def turn(e):
        pltpu.make_async_copy(land.at[e], land.at[e], a2a_recv.at[e]).wait()
        turned[:, e] = jnp.swapaxes(land[e].astype(F32), 0, 1).astype(BF16)

    stages = (low, relay, finish, forward, gradient, turn)

    def step(s, _):
        for lag, stage in enumerate(stages):

            @pl.when(jnp.logical_and(s >= lag, s < lag + SEQ))
            def _(lag=lag, stage=stage):
                stage(s - lag)

        return 0

    lax.fori_loop(0, SEQ + len(stages) - 1, step, 0)

    block_load.wait()

    def project(n, _):
        o_core, o_chip, i = n // 32, (n // 2) % 16, n % 2
        o = ((o_chip // 2) * 4 + o_core * 2 + o_chip % 2) * 2 + i
        picked = turned[rows[o]].reshape(SEQ * GROUPS, 256)
        contrib[o_core, o_chip, i] = jnp.dot(picked, b_buf[o], preferred_element_type=F32)
        return 0

    lax.fori_loop(0, 64, project, 0)

    sibling = group + 2 - 4 * core
    swap = remote(contrib.at[1 - core], cross, cross_sem.at[0], cross_sem.at[1], sibling, me)
    swap.start()
    swap.wait()

    def add(p, _):
        summed[p] = (contrib[core, p] + cross[p]).astype(BF16)
        return 0

    lax.fori_loop(0, CHIPS, add, 0)

    def plane_copy(k):
        y, x = (yy + k // 4) % 4, (xx + k % 4) % 4
        to = (y // 2 * 4 + x) * 2 + y % 2
        return remote(
            summed.at[to], plane.at[k], plane_send.at[k], plane_recv.at[k], group_of(y, x, core), me
        )

    def plane_start(k, _):
        plane_copy(k).start()
        return 0

    lax.fori_loop(1, CHIPS, plane_start, 0)
    contrib[core, chip] = contrib[core, chip] + cross[chip]

    def plane_add(k, _):
        plane_copy(k).wait_recv()
        contrib[core, chip] = contrib[core, chip] + plane[k].astype(F32)
        return 0

    lax.fori_loop(1, CHIPS, plane_add, 0)

    for i in range(2):
        for e in range(SEQ):
            fsend[:, i, e, :] = contrib[core, chip, i, e * 32 : e * 32 + 32, :]

    def is_self(s):
        return jnp.logical_and(s == group, goal == me)

    def final_copy(s):
        slot = (group % 8) * 4 + me
        return remote(fsend.at[s], frecv.at[slot], fin_send, fin_recv, s, goal)

    def final_start(s, _):
        @pl.when(is_self(s))
        def _():
            slot = (group % 8) * 4 + me
            pltpu.make_async_copy(fsend.at[s], frecv.at[slot], fin_recv).start()

        @pl.when(jnp.logical_not(is_self(s)))
        def _():
            final_copy(s).start()

        return 0

    lax.fori_loop(0, GROUPS, final_start, 0)
    pltpu.make_async_copy(frecv, frecv, fin_recv).wait()
    for n in range(8):
        out[2 * n : 2 * n + 2] = (frecv[4 * n] + frecv[4 * n + 1]) + (frecv[4 * n + 2] + frecv[4 * n + 3])

    def drain(e, _):
        for n in range(6):
            rs_copy(e, n).wait_send()
            ag_copy(e, n).wait_send()
        pltpu.make_async_copy(
            land.at[e, pl.ds(0, 31)], land.at[e, pl.ds(0, 31)], a2a_send.at[e]
        ).wait()
        return 0

    lax.fori_loop(0, SEQ, drain, 0)

    def plane_drain(k, _):
        plane_copy(k).wait_send()
        return 0

    lax.fori_loop(1, CHIPS, plane_drain, 0)

    def final_drain(s, _):
        @pl.when(jnp.logical_not(is_self(s)))
        def _():
            final_copy(s).wait_send()

        return 0

    lax.fori_loop(0, GROUPS, final_drain, 0)


def local(acts, cotangent, adapter_down, adapter_up, lengths, projection_rows, projection_blocks):
    vmem, smem, hbm = (pl.BlockSpec(memory_space=m) for m in (pltpu.VMEM, pltpu.SMEM, pl.ANY))
    dma = pltpu.SemaphoreType.DMA
    out = pl.pallas_call(
        kernel,
        out_shape=jax.ShapeDtypeStruct((16, 8, 128), F32),
        in_specs=[hbm, hbm, vmem, vmem, smem, smem, hbm],
        out_specs=vmem,
        scratch_shapes=[
            pltpu.VMEM((SEQ, 4, 256, 1024), BF16),
            pltpu.VMEM((SEQ, 4, 256, 1024), BF16),
            pltpu.VMEM((64, 256, 128), BF16),
            pltpu.VMEM((SEQ, 256, 256), F32),
            pltpu.VMEM((SEQ, 2, 128, 256), F32),
            pltpu.VMEM((SEQ, 4, 2, 128, 256), BF16),
            pltpu.VMEM((SEQ, 2, 128, 256), BF16),
            pltpu.VMEM((SEQ, 4, 128, 256), BF16),
            pltpu.VMEM((SEQ, 8, 128, 256), BF16),
            pltpu.VMEM((SEQ, 32, 32, 256), BF16),
            pltpu.VMEM((SEQ, 32, 32, 256), BF16),
            pltpu.VMEM((32, SEQ, 32, 256), BF16),
            pltpu.VMEM((2, CHIPS, 2, SEQ * GROUPS, 128), F32),
            pltpu.VMEM((CHIPS, 2, SEQ * GROUPS, 128), F32),
            pltpu.VMEM((CHIPS, 2, SEQ * GROUPS, 128), BF16),
            pltpu.VMEM((CHIPS, 2, SEQ * GROUPS, 128), BF16),
            pltpu.VMEM((GROUPS, 2, 8, 128), F32),
            pltpu.VMEM((32, 2, 8, 128), F32),
            dma((2, SEQ)), dma, dma((SEQ, 6)), dma((SEQ, 6)), dma((SEQ, 6)), dma((SEQ, 6)), dma((SEQ,)), dma((SEQ,)),
            dma((2,)), dma((CHIPS,)), dma((CHIPS,)), dma, dma,
        ],
        compiler_params=pltpu.CompilerParams(
            collective_id=0, has_side_effects=True, vmem_limit_bytes=60 * 1024 * 1024
        ),
        cost_estimate=pl.CostEstimate(flops=6 * 10**9, bytes_accessed=25 * 10**6, transcendentals=0),
    )(
        acts.reshape(SEQ, 4, 256, 1024),
        cotangent.reshape(SEQ, 4, 256, 1024),
        adapter_down,
        adapter_up,
        lengths,
        projection_rows.reshape(64),
        projection_blocks.reshape(64, 256, 128),
    )
    return jnp.swapaxes(out, 0, 1)[:SEQ].reshape(SEQ, 2048)


def solution(mesh):
    placed = (
        P(("dp", "proj"), None, "tensor"),
        P(("dp", "proj"), None, "tensor"),
        P("tensor", None),
        P(None, "tensor"),
        P(("dp", "proj")),
        P("tensor", ("dp", "proj"), None),
        P("tensor", ("dp", "proj"), None, None, None),
    )
    return jax.shard_map(
        local, mesh=mesh, in_specs=placed, out_specs=P(("dp", "proj"), "tensor"), check_vma=False
    )
```

time: 370 us -> 124 us (0.34)
  waiting for transfers between devices: 298 us -> 0 us
  Pallas kernels: 0 us -> 122 us
  matrix products: 27.9 us -> 0 us
  local copies, waits for them, and re-layouts: 20.8 us -> 1.47 us
  between operations: 13.9 us -> 0.01 us
  starting transfers between devices: 8.02 us -> 0 us
    pallas_call x0 -> x1, Pallas kernels: none -> 122 us  [local(): pl.pallas_call(kernel, out_shape=jax.ShapeDtypeStruct((16, 8, 128), F32),...]
    psum x1 -> x0, waiting for transfers between devices: 113 us -> none  [local(): h_total, u_total = lax.psum((reduced_hidden, reduced_upstream), 'tensor')]
    unnamed x4 -> x0, waiting for transfers between devices: 111 us -> none
    all_to_all x1 -> x0, waiting for transfers between devices: 54.3 us -> none  [local(): lax.all_to_all(direct_gradient, ('dp', 'proj'), split_axis=2, concat_axis...]
    dot_general x5 -> x0, matrix products: 27.9 us -> none  [the longest x1 8.5 us: local(): jnp.einsum('spu,un->spn', acts, adapter_down, preferred_element_type=jnp....]
    reduce_scatter x1 -> x0, waiting for transfers between devices: 19 us -> none  [local(): lax.psum_scatter(own_rows, 'tensor', scatter_dimension=1, tiled=True)]
    all_to_all x1 -> x0, starting transfers between devices: 7.76 us -> none  [local(): lax.all_to_all(direct_gradient, ('dp', 'proj'), split_axis=2, concat_axis...]
    unnamed x24 -> x0, local copies, waits for them, and re-layouts: 5.28 us -> none
  transfers between devices with their start and end apart: 4 -> 0, of which waited for: 4 -> 0; matrix products, arithmetic and copies ran while one was open for 0% -> 0% of each run, Pallas kernels for 0% -> 0%
where the time goes in v1:
time: 124 us; the launch traced here: 123 us
  Pallas kernels  122 us (98%)
  local copies, waits for them, and re-layouts  1.47 us (1%)
    pallas_call x1, Pallas kernels, local(): pl.pallas_call(kernel, out_shape=jax.ShapeDtypeStruct((16, 8, 128), F32),...  122 us

profile of v1, /device:TPU:1, one launch (start us, length us, event | category | flops | bytes accessed | tf_op | source)
XLA Modules:
  0.0 123.4 jit_solution(16859343442503714926)
XLA Ops:
  0.0 121.9 %shard_map.73 = f32[16,8,128]{2,1,0:T(8,128)} custom-call(bf16[5,4,256,1024]{3,2,1,0:T(8,128)(2,1)} %bitcast.7, bf16[5,4,256,1024]{3,2,1,0:T(8,128)(2,1)} %bitcast.8, bf16[1024,128]{1,0:T(8,128)(2,1)} %down.1, bf16[128,1024]{1,0:T(8,128)(2,1)} %up.1, s32[5]{0:T(128)} %lens.1, s32[64]{0:T(128)} %bitcast.11, bf16[64,256,128]{2,1,0:T(8,128)(2,1)} %bitcast.9), custom_call_target="tpu_custom_call" | custom-call | flops 6000000000 | bytes 25000000 | tf_op jit(solution)/shard_map/pallas_call | solution.py:313
  122.0 1.5 %slice_bitcast_fusion = f32[5,2048]{1,0:T(8,128)} fusion(f32[8,16,128]{2,0,1:T(8,128)} %bitcast.10), kind=kLoop, calls=%fused_computation | loop fusion | bytes 81920 | tf_op jit(solution)/shard_map/reshape | solution.py:353

commit v2 on v1

v2 whole, which is shorter than its diff:
```python
import functools

import jax
import jax.numpy as jnp
from jax import lax
from jax.experimental import pallas as pl
from jax.experimental.pallas import tpu as pltpu
from jax.sharding import PartitionSpec as P

MESH = pl.DeviceIdType.MESH
F32 = jnp.float32
BF16 = jnp.bfloat16
SEQ = 5
CHIPS = 16


SHIFTS = (
    (1, 0), (0, 1), (3, 0), (0, 3), (1, 1), (3, 3), (1, 3), (3, 1),
    (2, 0), (0, 2), (2, 1), (1, 2), (2, 3), (3, 2), (2, 2),
)
PEERS = ((0, 0, 1),) + tuple((x, y, c) for x, y in SHIFTS for c in (0, 1))


def kernel(
    acts, cot, down, up, lens, rows, blocks, out,
    a_buf, c_buf, b_buf, own, relay_f, part, relay_in, fin_in, gath, grads, land, turned,
    contrib, cross, swapped, summed, mine, plane, fsend, frecv,
    load_sem, block_sem, rs_send, rs_recv, ag_send, ag_recv, a2a_send, a2a_recv,
    cross_send, cross_recv, plane_send, plane_recv, fin_send, fin_recv,
):
    dp, pj, me = lax.axis_index("dp"), lax.axis_index("proj"), lax.axis_index("tensor")
    group = dp * 2 + pj
    core = lax.rem(dp, 2)
    xx = lax.rem(lax.div(dp, 2), 4)
    yy = lax.div(dp, 8) * 2 + pj
    xs = [lax.rem(xx + d, 4) for d in range(4)]
    ys = [lax.rem(yy + d, 4) for d in range(4)]
    yh = [lax.div(y, 2) for y in ys]
    yl = [lax.rem(y, 2) for y in ys]
    cores = (core, 1 - core)
    z_at = [lax.rem(me + d, 4) for d in range(4)]
    right, far, left = z_at[1:]

    def device(x, y, c, z=0):
        return {"dp": yh[y] * 8 + xs[x] * 2 + cores[c], "proj": yl[y], "tensor": z_at[z]}

    def rank(x, y, c):
        return (yh[y] * 8 + xs[x] * 2 + cores[c]) * 2 + yl[y]

    def chip_at(x, y):
        return (yh[y] * 4 + xs[x]) * 2 + yl[y]

    place = chip_at(0, 0) * 2 + core

    def loads(e):
        return (
            pltpu.make_async_copy(acts.at[e], a_buf.at[e], load_sem.at[0, e]),
            pltpu.make_async_copy(cot.at[e], c_buf.at[e], load_sem.at[1, e]),
        )

    for e in range(SEQ):
        for copy in loads(e):
            copy.start()
    block_load = pltpu.make_async_copy(blocks, b_buf, block_sem)
    block_load.start()

    barrier = pltpu.get_barrier_semaphore()
    others = [device(x, y, c) for x, y, c in PEERS] + [device(0, 0, c, z) for c in (0, 1) for z in (1, 2, 3)]
    for other in others:
        pl.semaphore_signal(barrier, inc=1, device_id=other, device_id_type=MESH)
    pl.semaphore_wait(barrier, len(others))

    def remote(src, dst, send, recv, to):
        return pltpu.make_async_remote_copy(
            src_ref=src, dst_ref=dst, send_sem=send, recv_sem=recv, device_id=to, device_id_type=MESH
        )

    def rs_copy(e, n):
        src, dst, z = (
            lambda: (part.at[e, far, 0], relay_in.at[e, 1], 3),
            lambda: (part.at[e, far, 1], relay_in.at[e, 0], 1),
            lambda: (part.at[e, right, 0], fin_in.at[e, 0], 1),
            lambda: (part.at[e, left, 1], fin_in.at[e, 3], 3),
            lambda: (part.at[e, right, 1], fin_in.at[e, 1], 1),
            lambda: (part.at[e, left, 0], fin_in.at[e, 2], 3),
        )[n]()
        return remote(src, dst, rs_send.at[e, n], rs_recv.at[e, n], device(0, 0, 0, z))

    def ag_copy(e, n):
        q, half, z = ((me, 0, 1), (me, 1, 3), (me, 1, 1), (me, 0, 3), (left, 0, 1), (right, 1, 3))[n]
        block = gath.at[e, q * 2 + half]
        return remote(block, block, ag_send.at[e, n], ag_recv.at[e, n], device(0, 0, 0, z))

    def low(e):
        for copy in loads(e):
            copy.wait()

        def partial(q):
            h = jnp.dot(a_buf[e, q], down[...], preferred_element_type=F32)
            u = lax.dot_general(c_buf[e, q], up[...], (((1,), (1,)), ((), ())), preferred_element_type=F32)
            return h, u

        h, u = partial(far)
        part[e, far, :, :, 0:128] = h.astype(BF16).reshape(2, 128, 128)
        part[e, far, :, :, 128:256] = u.astype(BF16).reshape(2, 128, 128)
        rs_copy(e, 0).start()
        rs_copy(e, 1).start()
        h, u = partial(right)
        part[e, right, 0, :, 0:128] = h[0:128].astype(BF16)
        part[e, right, 0, :, 128:256] = u[0:128].astype(BF16)
        relay_f[e, 0, :, 0:128] = h[128:256]
        relay_f[e, 0, :, 128:256] = u[128:256]
        rs_copy(e, 2).start()
        h, u = partial(left)
        part[e, left, 1, :, 0:128] = h[128:256].astype(BF16)
        part[e, left, 1, :, 128:256] = u[128:256].astype(BF16)
        relay_f[e, 1, :, 0:128] = h[0:128]
        relay_f[e, 1, :, 128:256] = u[0:128]
        rs_copy(e, 3).start()
        h, u = partial(me)
        own[e, :, 0:128] = h
        own[e, :, 128:256] = u

    def relay(e):
        rs_copy(e, 1).wait_recv()
        part[e, right, 1] = (relay_f[e, 0] + relay_in[e, 0].astype(F32)).astype(BF16)
        rs_copy(e, 4).start()
        rs_copy(e, 0).wait_recv()
        part[e, left, 0] = (relay_f[e, 1] + relay_in[e, 1].astype(F32)).astype(BF16)
        rs_copy(e, 5).start()

    def finish(e):
        length = jnp.full((128, 256), lens[e], jnp.int32)

        def half(n, first, second):
            token = lax.broadcasted_iota(jnp.int32, (128, 256), 0) + (me * 256 + n * 128)
            weight = jnp.where(token < length, 1.0 / length.astype(F32), 0.0)
            total = own[e, n * 128 : n * 128 + 128] + (fin_in[e, first].astype(F32) + fin_in[e, second].astype(F32))
            gath[e, me * 2 + n] = (total * weight).astype(BF16)

        rs_copy(e, 2).wait_recv()
        rs_copy(e, 5).wait_recv()
        half(0, 0, 2)
        ag_copy(e, 0).start()
        rs_copy(e, 3).wait_recv()
        rs_copy(e, 4).wait_recv()
        half(1, 3, 1)
        ag_copy(e, 1).start()
        ag_copy(e, 2).start()
        ag_copy(e, 3).start()

    def forward(e):
        ag_copy(e, 0).wait_recv()
        ag_copy(e, 4).start()
        ag_copy(e, 1).wait_recv()
        ag_copy(e, 5).start()

    def gradient(e):
        for n in (2, 3, 4, 5):
            ag_copy(e, n).wait_recv()
        for side in (0, 1):
            buf = (a_buf, c_buf)[side]
            other = gath[e, :, :, 128 - side * 128 : 256 - side * 128].reshape(1024, 128).T
            for w in range(4):
                wide = buf[e, :, :, w * 256 : w * 256 + 256].reshape(1024, 256)
                g = jnp.dot(other, wide, preferred_element_type=F32).T
                grads[e, w * 8 : w * 8 + 8, :, side * 128 : side * 128 + 128] = g.astype(BF16).reshape(8, 32, 128)
        pltpu.make_async_copy(grads.at[e, group], land.at[e, place], a2a_recv.at[e]).start()
        for x, y, c in PEERS:
            remote(
                grads.at[e, rank(x, y, c)], land.at[e, place], a2a_send.at[e], a2a_recv.at[e], device(x, y, c)
            ).start()

    def swap(e):
        return remote(
            contrib.at[e, 1 - core], cross.at[e], cross_send.at[e], cross_recv.at[e], device(0, 0, 1)
        )

    def project(e):
        pltpu.make_async_copy(land.at[e], land.at[e], a2a_recv.at[e]).wait()
        turned[...] = jnp.swapaxes(land[e].astype(F32), 0, 1).astype(BF16)

        def half(h):
            def one(n, _):
                o = lax.div(n, 8) * 16 + h * 8 + lax.rem(n, 8)
                contrib[e, h, n] = jnp.dot(turned[rows[o]], b_buf[o], preferred_element_type=F32)
                return 0

            lax.fori_loop(0, 32, one, 0, unroll=16)

        half(1 - core)
        swap(e).start()
        half(core)

    def scatter(e):
        swap(e).wait_recv()
        swapped[...] = jnp.swapaxes(contrib[e, core] + cross[e], 0, 1)
        summed[e] = swapped[...].astype(BF16).reshape(CHIPS, 2, 32, 128)
        for k, (x, y) in enumerate(SHIFTS):
            remote(
                summed.at[e, chip_at(x, y)], plane.at[e, k], plane_send.at[e], plane_recv.at[e], device(x, y, 0)
            ).start()
        for k in range(2):
            mine[e, k] = swapped[chip_at(0, 0) * 2 + k]

    def collect(e):
        pltpu.make_async_copy(plane.at[e], plane.at[e], plane_recv.at[e]).wait()
        total = mine[e]
        for k in range(len(SHIFTS)):
            total = total + plane[e, k].astype(F32)
        fsend[e] = total.reshape(2, 4, 8, 128)
        for c in (0, 1):
            for z in range(4):
                src, dst = fsend.at[e, cores[c], z_at[z]], frecv.at[e, core, me]
                if c == 0 and z == 0:
                    pltpu.make_async_copy(src, dst, fin_recv.at[e]).start()
                else:
                    remote(src, dst, fin_send.at[e], fin_recv.at[e], device(0, 0, c, z)).start()

    stages = (low, relay, finish, forward, gradient, project, scatter, collect)

    def step(s, _):
        @pl.when(s == 5)
        def _():
            block_load.wait()

        for lag, stage in enumerate(stages):

            @pl.when(jnp.logical_and(s >= lag, s < lag + SEQ))
            def _(lag=lag, stage=stage):
                stage(s - lag)

        return 0

    lax.fori_loop(0, SEQ + len(stages) - 1, step, 0)

    for e in range(SEQ):
        pltpu.make_async_copy(frecv.at[e], frecv.at[e], fin_recv.at[e]).wait()
        for h in range(2):
            out[e, h * 8 : h * 8 + 8] = (frecv[e, h, 0] + frecv[e, h, 1]) + (frecv[e, h, 2] + frecv[e, h, 3])

    def drain(e, _):
        for n in range(6):
            rs_copy(e, n).wait_send()
            ag_copy(e, n).wait_send()
        swap(e).wait_send()
        for ref, sem in (
            (land.at[e, pl.ds(0, 31)], a2a_send.at[e]),
            (plane.at[e], plane_send.at[e]),
            (fsend.at[e, 0, pl.ds(0, 3)], fin_send.at[e]),
            (fsend.at[e, 1], fin_send.at[e]),
        ):
            pltpu.make_async_copy(ref, ref, sem).wait()
        return 0

    lax.fori_loop(0, SEQ, drain, 0)


def local(acts, cotangent, adapter_down, adapter_up, lengths, projection_rows, projection_blocks):
    vmem, smem, hbm = (pl.BlockSpec(memory_space=m) for m in (pltpu.VMEM, pltpu.SMEM, pl.ANY))
    dma = pltpu.SemaphoreType.DMA
    out = pl.pallas_call(
        kernel,
        out_shape=jax.ShapeDtypeStruct((SEQ, 16, 128), F32),
        in_specs=[hbm, hbm, vmem, vmem, smem, smem, hbm],
        out_specs=vmem,
        scratch_shapes=[
            pltpu.VMEM((SEQ, 4, 256, 1024), BF16),
            pltpu.VMEM((SEQ, 4, 256, 1024), BF16),
            pltpu.VMEM((64, 256, 128), BF16),
            pltpu.VMEM((SEQ, 256, 256), F32),
            pltpu.VMEM((SEQ, 2, 128, 256), F32),
            pltpu.VMEM((SEQ, 4, 2, 128, 256), BF16),
            pltpu.VMEM((SEQ, 2, 128, 256), BF16),
            pltpu.VMEM((SEQ, 4, 128, 256), BF16),
            pltpu.VMEM((SEQ, 8, 128, 256), BF16),
            pltpu.VMEM((SEQ, 32, 32, 256), BF16),
            pltpu.VMEM((SEQ, 32, 32, 256), BF16),
            pltpu.VMEM((32, 32, 256), BF16),
            pltpu.VMEM((SEQ, 2, 32, 32, 128), F32),
            pltpu.VMEM((SEQ, 32, 32, 128), F32),
            pltpu.VMEM((32, 32, 128), F32),
            pltpu.VMEM((SEQ, CHIPS, 2, 32, 128), BF16),
            pltpu.VMEM((SEQ, 2, 32, 128), F32),
            pltpu.VMEM((SEQ, CHIPS - 1, 2, 32, 128), BF16),
            pltpu.VMEM((SEQ, 2, 4, 8, 128), F32),
            pltpu.VMEM((SEQ, 2, 4, 8, 128), F32),
            dma((2, SEQ)), dma, dma((SEQ, 6)), dma((SEQ, 6)), dma((SEQ, 6)), dma((SEQ, 6)), dma((SEQ,)), dma((SEQ,)),
            dma((SEQ,)), dma((SEQ,)), dma((SEQ,)), dma((SEQ,)), dma((SEQ,)), dma((SEQ,)),
        ],
        compiler_params=pltpu.CompilerParams(
            collective_id=0, has_side_effects=True, vmem_limit_bytes=60 * 1024 * 1024
        ),
        cost_estimate=pl.CostEstimate(flops=6 * 10**9, bytes_accessed=25 * 10**6, transcendentals=0),
    )(
        acts.reshape(SEQ, 4, 256, 1024),
        cotangent.reshape(SEQ, 4, 256, 1024),
        adapter_down,
        adapter_up,
        lengths,
        projection_rows.reshape(64),
        projection_blocks.reshape(64, 256, 128),
    )
    return out.reshape(SEQ, 2048)


def solution(mesh):
    placed = (
        P(("dp", "proj"), None, "tensor"),
        P(("dp", "proj"), None, "tensor"),
        P("tensor", None),
        P(None, "tensor"),
        P(("dp", "proj")),
        P("tensor", ("dp", "proj"), None),
        P("tensor", ("dp", "proj"), None, None, None),
    )
    return jax.shard_map(
        local, mesh=mesh, in_specs=placed, out_specs=P(("dp", "proj"), "tensor"), check_vma=False
    )
```

time: 124 us -> 96.3 us (0.78)
  Pallas kernels: 122 us -> 94.7 us
    pallas_call x1, Pallas kernels: 122 us -> 94.7 us  [local(): pl.pallas_call(kernel, out_shape=jax.ShapeDtypeStruct((SEQ, 16, 128), F32...]
    reshape x1 -> x0, local copies, waits for them, and re-layouts: 1.47 us -> none  [local(): return jnp.swapaxes(out, 0, 1)[:SEQ].reshape(SEQ, 2048)]
    unnamed x0 -> x1, local copies, waits for them, and re-layouts: none -> 1.43 us
where the time goes in v2:
time: 96.3 us; the launch traced here: 96.1 us
  Pallas kernels  94.7 us (98%)
  local copies, waits for them, and re-layouts  1.43 us (1%)
    pallas_call x1, Pallas kernels, local(): pl.pallas_call(kernel, out_shape=jax.ShapeDtypeStruct((SEQ, 16, 128), F32...  94.7 us

profile of v2, /device:TPU:1, one launch (start us, length us, event | category | flops | bytes accessed | tf_op | source)
XLA Modules:
  0.0 96.1 jit_solution(11051600694626430007)
XLA Ops:
  0.0 94.7 %shard_map.73 = f32[5,16,128]{2,1,0:T(8,128)} custom-call(bf16[5,4,256,1024]{3,2,1,0:T(8,128)(2,1)} %bitcast.8, bf16[5,4,256,1024]{3,2,1,0:T(8,128)(2,1)} %bitcast.9, bf16[1024,128]{1,0:T(8,128)(2,1)} %down.1, bf16[128,1024]{1,0:T(8,128)(2,1)} %up.1, s32[5]{0:T(128)} %lens.1, s32[64]{0:T(128)} %bitcast.12, bf16[64,256,128]{2,1,0:T(8,128)(2,1)} %bitcast.10), custom_call_target="tpu_custom_call" | custom-call | flops 6000000000 | bytes 25000000 | tf_op jit(solution)/shard_map/pallas_call | solution.py:262
  94.7 1.4 %copy.10 = f32[1,5,16,128]{3,1,2,0:T(8,128)} copy(f32[1,5,16,128]{3,2,1,0:T(8,128)} %bitcast.11) | data formatting | bytes 81920

commit v3 on v2

--- a/solution.py
+++ b/solution.py
@@ -15,10 +15,10 @@
 
 
 SHIFTS = (
-    (1, 0), (0, 1), (3, 0), (0, 3), (1, 1), (3, 3), (1, 3), (3, 1),
-    (2, 0), (0, 2), (2, 1), (1, 2), (2, 3), (3, 2), (2, 2),
+    (2, 2), (3, 2), (2, 3), (1, 2), (2, 1), (0, 2), (2, 0), (3, 1),
+    (1, 3), (3, 3), (1, 1), (0, 3), (3, 0), (0, 1), (1, 0),
 )
-PEERS = ((0, 0, 1),) + tuple((x, y, c) for x, y in SHIFTS for c in (0, 1))
+PEERS = tuple((x, y, c) for x, y in SHIFTS for c in (0, 1)) + ((0, 0, 1),)
 
 
 def kernel(
@@ -58,17 +58,18 @@
             pltpu.make_async_copy(cot.at[e], c_buf.at[e], load_sem.at[1, e]),
         )
 
-    for e in range(SEQ):
-        for copy in loads(e):
-            copy.start()
+    for copy in loads(0):
+        copy.start()
     block_load = pltpu.make_async_copy(blocks, b_buf, block_sem)
-    block_load.start()
 
     barrier = pltpu.get_barrier_semaphore()
     others = [device(x, y, c) for x, y, c in PEERS] + [device(0, 0, c, z) for c in (0, 1) for z in (1, 2, 3)]
     for other in others:
         pl.semaphore_signal(barrier, inc=1, device_id=other, device_id_type=MESH)
-    pl.semaphore_wait(barrier, len(others))
+    for e in range(1, SEQ):
+        for copy in loads(e):
+            copy.start()
+    block_load.start()
 
     def remote(src, dst, send, recv, to):
         return pltpu.make_async_remote_copy(
@@ -86,38 +87,47 @@
         )[n]()
         return remote(src, dst, rs_send.at[e, n], rs_recv.at[e, n], device(0, 0, 0, z))
 
-    def ag_copy(e, n):
-        q, half, z = ((me, 0, 1), (me, 1, 3), (me, 1, 1), (me, 0, 3), (left, 0, 1), (right, 1, 3))[n]
-        block = gath.at[e, q * 2 + half]
-        return remote(block, block, ag_send.at[e, n], ag_recv.at[e, n], device(0, 0, 0, z))
-
-    def low(e):
+    def ag_copy(e, z):
+        return remote(
+            gath.at[e, me], gath.at[e, me], ag_send.at[e, z - 1], ag_recv.at[e, z - 1], device(0, 0, 0, z)
+        )
+
+    def partial(e, q):
+        h = jnp.dot(a_buf[e, q], down[...], preferred_element_type=F32)
+        u = lax.dot_general(c_buf[e, q], up[...], (((1,), (1,)), ((), ())), preferred_element_type=F32)
+        return h, u
+
+    def far_sums(e):
         for copy in loads(e):
             copy.wait()
-
-        def partial(q):
-            h = jnp.dot(a_buf[e, q], down[...], preferred_element_type=F32)
-            u = lax.dot_general(c_buf[e, q], up[...], (((1,), (1,)), ((), ())), preferred_element_type=F32)
-            return h, u
-
-        h, u = partial(far)
+        h, u = partial(e, far)
         part[e, far, :, :, 0:128] = h.astype(BF16).reshape(2, 128, 128)
         part[e, far, :, :, 128:256] = u.astype(BF16).reshape(2, 128, 128)
-        rs_copy(e, 0).start()
-        rs_copy(e, 1).start()
-        h, u = partial(right)
+
+    def near_sums(e):
+        h, u = partial(e, right)
         part[e, right, 0, :, 0:128] = h[0:128].astype(BF16)
         part[e, right, 0, :, 128:256] = u[0:128].astype(BF16)
         relay_f[e, 0, :, 0:128] = h[128:256]
         relay_f[e, 0, :, 128:256] = u[128:256]
-        rs_copy(e, 2).start()
-        h, u = partial(left)
+        h, u = partial(e, left)
         part[e, left, 1, :, 0:128] = h[128:256].astype(BF16)
         part[e, left, 1, :, 128:256] = u[128:256].astype(BF16)
         relay_f[e, 1, :, 0:128] = h[0:128]
         relay_f[e, 1, :, 128:256] = u[0:128]
+
+    def low_far(e):
+        if e:
+            far_sums(e)
+        rs_copy(e, 0).start()
+        rs_copy(e, 1).start()
+
+    def low_near(e):
+        if e:
+            near_sums(e)
+        rs_copy(e, 2).start()
         rs_copy(e, 3).start()
-        h, u = partial(me)
+        h, u = partial(e, me)
         own[e, :, 0:128] = h
         own[e, :, 128:256] = u
 
@@ -136,28 +146,18 @@
             token = lax.broadcasted_iota(jnp.int32, (128, 256), 0) + (me * 256 + n * 128)
             weight = jnp.where(token < length, 1.0 / length.astype(F32), 0.0)
             total = own[e, n * 128 : n * 128 + 128] + (fin_in[e, first].astype(F32) + fin_in[e, second].astype(F32))
-            gath[e, me * 2 + n] = (total * weight).astype(BF16)
-
-        rs_copy(e, 2).wait_recv()
-        rs_copy(e, 5).wait_recv()
+            gath[e, me, n * 128 : n * 128 + 128] = (total * weight).astype(BF16)
+
+        for n in (2, 5, 3, 4):
+            rs_copy(e, n).wait_recv()
         half(0, 0, 2)
-        ag_copy(e, 0).start()
-        rs_copy(e, 3).wait_recv()
-        rs_copy(e, 4).wait_recv()
         half(1, 3, 1)
-        ag_copy(e, 1).start()
-        ag_copy(e, 2).start()
-        ag_copy(e, 3).start()
-
-    def forward(e):
-        ag_copy(e, 0).wait_recv()
-        ag_copy(e, 4).start()
-        ag_copy(e, 1).wait_recv()
-        ag_copy(e, 5).start()
+        for z in (2, 1, 3):
+            ag_copy(e, z).start()
 
     def gradient(e):
-        for n in (2, 3, 4, 5):
-            ag_copy(e, n).wait_recv()
+        for z in (1, 3, 2):
+            ag_copy(e, z).wait_recv()
         for side in (0, 1):
             buf = (a_buf, c_buf)[side]
             other = gath[e, :, :, 128 - side * 128 : 256 - side * 128].reshape(1024, 128).T
@@ -175,6 +175,9 @@
         return remote(
             contrib.at[e, 1 - core], cross.at[e], cross_send.at[e], cross_recv.at[e], device(0, 0, 1)
         )
+
+    def blocks_ready(_):
+        block_load.wait()
 
     def project(e):
         pltpu.make_async_copy(land.at[e], land.at[e], a2a_recv.at[e]).wait()
@@ -217,22 +220,20 @@
                 else:
                     remote(src, dst, fin_send.at[e], fin_recv.at[e], device(0, 0, c, z)).start()
 
-    stages = (low, relay, finish, forward, gradient, project, scatter, collect)
-
-    def step(s, _):
-        @pl.when(s == 5)
-        def _():
-            block_load.wait()
-
-        for lag, stage in enumerate(stages):
-
-            @pl.when(jnp.logical_and(s >= lag, s < lag + SEQ))
-            def _(lag=lag, stage=stage):
-                stage(s - lag)
-
-        return 0
-
-    lax.fori_loop(0, SEQ + len(stages) - 1, step, 0)
+    far_sums(0)
+    near_sums(0)
+    pl.semaphore_wait(barrier, len(others))
+
+    order = (
+        (low_far, 0), (low_near, 0), (low_far, 1), (relay, 0), (low_near, 1), (relay, 1), (finish, 0),
+        (low_far, 2), (finish, 1), (low_near, 2), (gradient, 0), (relay, 2), (low_far, 3), (low_near, 3),
+        (gradient, 1), (finish, 2), (low_far, 4), (relay, 3), (blocks_ready, 0), (project, 0), (low_near, 4),
+        (scatter, 0), (relay, 4), (gradient, 2), (finish, 3), (project, 1), (scatter, 1), (finish, 4),
+        (collect, 0), (gradient, 3), (gradient, 4), (project, 2), (collect, 1), (scatter, 2), (project, 3),
+        (scatter, 3), (project, 4), (scatter, 4), (collect, 2), (collect, 3), (collect, 4),
+    )
+    for stage, e in order:
+        stage(e)
 
     for e in range(SEQ):
         pltpu.make_async_copy(frecv.at[e], frecv.at[e], fin_recv.at[e]).wait()
@@ -242,7 +243,8 @@
     def drain(e, _):
         for n in range(6):
             rs_copy(e, n).wait_send()
-            ag_copy(e, n).wait_send()
+        for z in (1, 2, 3):
+            ag_copy(e, z).wait_send()
         swap(e).wait_send()
         for ref, sem in (
             (land.at[e, pl.ds(0, 31)], a2a_send.at[e]),
@@ -273,7 +275,7 @@
             pltpu.VMEM((SEQ, 4, 2, 128, 256), BF16),
             pltpu.VMEM((SEQ, 2, 128, 256), BF16),
             pltpu.VMEM((SEQ, 4, 128, 256), BF16),
-            pltpu.VMEM((SEQ, 8, 128, 256), BF16),
+            pltpu.VMEM((SEQ, 4, 256, 256), BF16),
             pltpu.VMEM((SEQ, 32, 32, 256), BF16),
             pltpu.VMEM((SEQ, 32, 32, 256), BF16),
             pltpu.VMEM((32, 32, 256), BF16),
@@ -285,7 +287,7 @@
             pltpu.VMEM((SEQ, CHIPS - 1, 2, 32, 128), BF16),
             pltpu.VMEM((SEQ, 2, 4, 8, 128), F32),
             pltpu.VMEM((SEQ, 2, 4, 8, 128), F32),
-            dma((2, SEQ)), dma, dma((SEQ, 6)), dma((SEQ, 6)), dma((SEQ, 6)), dma((SEQ, 6)), dma((SEQ,)), dma((SEQ,)),
+            dma((2, SEQ)), dma, dma((SEQ, 6)), dma((SEQ, 6)), dma((SEQ, 3)), dma((SEQ, 3)), dma((SEQ,)), dma((SEQ,)),
             dma((SEQ,)), dma((SEQ,)), dma((SEQ,)), dma((SEQ,)), dma((SEQ,)), dma((SEQ,)),
         ],
         compiler_params=pltpu.CompilerParams(

time: 96.3 us -> 88.4 us (0.918)
  Pallas kernels: 94.7 us -> 86.8 us
    pallas_call x1, Pallas kernels: 94.7 us -> 86.8 us  [local(): pl.pallas_call(kernel, out_shape=jax.ShapeDtypeStruct((SEQ, 16, 128), F32...]
where the time goes in v3:
time: 88.4 us; the launch traced here: 88.3 us
  Pallas kernels  86.8 us (98%)
  local copies, waits for them, and re-layouts  1.43 us (2%)
    pallas_call x1, Pallas kernels, local(): pl.pallas_call(kernel, out_shape=jax.ShapeDtypeStruct((SEQ, 16, 128), F32...  86.8 us

profile of v3, /device:TPU:1, one launch (start us, length us, event | category | flops | bytes accessed | tf_op | source)
XLA Modules:
  0.0 88.3 jit_solution(17192453486703947935)
XLA Ops:
  0.0 86.8 %shard_map.73 = f32[5,16,128]{2,1,0:T(8,128)} custom-call(bf16[5,4,256,1024]{3,2,1,0:T(8,128)(2,1)} %bitcast.8, bf16[5,4,256,1024]{3,2,1,0:T(8,128)(2,1)} %bitcast.9, bf16[1024,128]{1,0:T(8,128)(2,1)} %down.1, bf16[128,1024]{1,0:T(8,128)(2,1)} %up.1, s32[5]{0:T(128)} %lens.1, s32[64]{0:T(128)} %bitcast.12, bf16[64,256,128]{2,1,0:T(8,128)(2,1)} %bitcast.10), custom_call_target="tpu_custom_call" | custom-call | flops 6000000000 | bytes 25000000 | tf_op jit(solution)/shard_map/pallas_call | solution.py:264
  86.8 1.4 %copy.10 = f32[1,5,16,128]{3,1,2,0:T(8,128)} copy(f32[1,5,16,128]{3,2,1,0:T(8,128)} %bitcast.11) | data formatting | bytes 81920

commit v4 on v3

v4 whole, which is shorter than its diff:
```python
import functools

import jax
import jax.numpy as jnp
from jax import lax
from jax.experimental import pallas as pl
from jax.experimental.pallas import tpu as pltpu
from jax.sharding import PartitionSpec as P

MESH = pl.DeviceIdType.MESH
F32 = jnp.float32
BF16 = jnp.bfloat16
SEQ = 5
UNITS = ((0, 0, 256), (1, 0, 256), (2, 0, 256), (3, 0, 256), (4, 0, 128), (4, 128, 128))
COUNT = len(UNITS)
STRAIGHT = (COUNT - 1,)
CHIPS = 16


SHIFTS = (
    (2, 2), (3, 2), (2, 3), (1, 2), (2, 1), (0, 2), (2, 0), (3, 1),
    (1, 3), (3, 3), (1, 1), (0, 3), (3, 0), (0, 1), (1, 0),
)
PEERS = tuple((x, y, c) for x, y in SHIFTS for c in (0, 1)) + ((0, 0, 1),)


def kernel(
    acts, cot, down_in, up_in, lens_in, rows_in, blocks, out,
    a_buf, c_buf, b_buf, down, up, lens, rows, own, relay_f, part, relay_in, fin_in, gath, grads, land, turned,
    contrib, cross, swapped, summed, mine, plane, fsend, frecv,
    load_sem, small_sem, block_sem, rs_send, rs_recv, ag_send, ag_recv, a2a_send, a2a_recv,
    cross_send, cross_recv, plane_send, plane_recv, fin_send, fin_recv,
):
    dp, pj, me = lax.axis_index("dp"), lax.axis_index("proj"), lax.axis_index("tensor")
    group = dp * 2 + pj
    core = lax.rem(dp, 2)
    xx = lax.rem(lax.div(dp, 2), 4)
    yy = lax.div(dp, 8) * 2 + pj
    xs = [lax.rem(xx + d, 4) for d in range(4)]
    ys = [lax.rem(yy + d, 4) for d in range(4)]
    yh = [lax.div(y, 2) for y in ys]
    yl = [lax.rem(y, 2) for y in ys]
    cores = (core, 1 - core)
    z_at = [lax.rem(me + d, 4) for d in range(4)]
    right, far, left = z_at[1:]

    def device(x, y, c, z=0):
        return {"dp": yh[y] * 8 + xs[x] * 2 + cores[c], "proj": yl[y], "tensor": z_at[z]}

    def rank(x, y, c):
        return (yh[y] * 8 + xs[x] * 2 + cores[c]) * 2 + yl[y]

    def chip_at(x, y):
        return (yh[y] * 4 + xs[x]) * 2 + yl[y]

    place = chip_at(0, 0) * 2 + core

    def loads(e):
        return (
            pltpu.make_async_copy(acts.at[e], a_buf.at[e], load_sem.at[0, e]),
            pltpu.make_async_copy(cot.at[e], c_buf.at[e], load_sem.at[1, e]),
        )

    small = [
        pltpu.make_async_copy(src, dst, small_sem.at[n])
        for n, (src, dst) in enumerate(((down_in, down), (up_in, up), (lens_in, lens), (rows_in, rows)))
    ]
    small[0].start()
    loads(0)[0].start()
    small[1].start()
    loads(0)[1].start()
    small[2].start()
    small[3].start()
    block_load = pltpu.make_async_copy(blocks, b_buf, block_sem)

    barrier = pltpu.get_barrier_semaphore()
    others = [device(x, y, c) for x, y, c in PEERS] + [device(0, 0, c, z) for c in (0, 1) for z in (1, 2, 3)]
    for other in others:
        pl.semaphore_signal(barrier, inc=1, device_id=other, device_id_type=MESH)
    for e in range(1, SEQ):
        for copy in loads(e):
            copy.start()
    block_load.start()

    def remote(src, dst, send, recv, to):
        return pltpu.make_async_remote_copy(
            src_ref=src, dst_ref=dst, send_sem=send, recv_sem=recv, device_id=to, device_id_type=MESH
        )

    def rs_copy(i, n):
        e, column, width = UNITS[i]
        q, half, ref, slot, z = (
            (far, 0, relay_in, 1, 3),
            (far, 1, relay_in, 0, 1),
            (right, 0, fin_in, 0, 1),
            (left, 1, fin_in, 3, 3),
            (right, 1, fin_in, 1, 1),
            (left, 0, fin_in, 2, 3),
        )[n]
        columns = pl.ds(column, width)
        return remote(
            part.at[e, q, half, :, columns], ref.at[e, slot, :, columns], rs_send.at[i, n], rs_recv.at[i, n],
            device(0, 0, 0, z),
        )

    def straight_copy(i, z):
        e, column, width = UNITS[i]
        block = gath.at[e, me, :, pl.ds(column, width)]
        return remote(block, block, ag_send.at[i, z - 1], ag_recv.at[i, z - 1], device(0, 0, 0, z))

    def ag_copy(i, n):
        e, column, width = UNITS[i]
        q, half, z = ((me, 0, 1), (me, 1, 3), (me, 1, 1), (me, 0, 3), (left, 0, 1), (right, 1, 3))[n]
        block = gath.at[e, q, pl.ds(half * 128, 128), pl.ds(column, width)]
        return remote(block, block, ag_send.at[i, n], ag_recv.at[i, n], device(0, 0, 0, z))

    def partial(i, q):
        e, column, width = UNITS[i]
        if column == 0:
            yield 0, jnp.dot(a_buf[e, q], down[...], preferred_element_type=F32)
        if column + width == 256:
            yield 128, lax.dot_general(c_buf[e, q], up[...], (((1,), (1,)), ((), ())), preferred_element_type=F32)

    def far_sums(i):
        e, column, width = UNITS[i]
        for side in range(column // 128, (column + width) // 128):
            loads(e)[side].wait()
        for c, value in partial(i, far):
            part[e, far, :, :, c : c + 128] = value.astype(BF16).reshape(2, 128, 128)

    def near_sums(i):
        e = UNITS[i][0]
        for c, value in partial(i, right):
            part[e, right, 0, :, c : c + 128] = value[0:128].astype(BF16)
            relay_f[e, 0, :, c : c + 128] = value[128:256]
        for c, value in partial(i, left):
            part[e, left, 1, :, c : c + 128] = value[128:256].astype(BF16)
            relay_f[e, 1, :, c : c + 128] = value[0:128]

    def low_far(i):
        if i:
            far_sums(i)
        rs_copy(i, 0).start()
        rs_copy(i, 1).start()

    def low_near(i):
        if i:
            near_sums(i)
        rs_copy(i, 2).start()
        rs_copy(i, 3).start()
        for c, value in partial(i, me):
            own[UNITS[i][0], :, c : c + 128] = value

    def relay(i):
        e, column, width = UNITS[i]
        to = column + width
        rs_copy(i, 1).wait_recv()
        part[e, right, 1, :, column:to] = (
            relay_f[e, 0, :, column:to] + relay_in[e, 0, :, column:to].astype(F32)
        ).astype(BF16)
        rs_copy(i, 4).start()
        rs_copy(i, 0).wait_recv()
        part[e, left, 0, :, column:to] = (
            relay_f[e, 1, :, column:to] + relay_in[e, 1, :, column:to].astype(F32)
        ).astype(BF16)
        rs_copy(i, 5).start()

    def finish(i):
        e, column, width = UNITS[i]
        to = column + width
        length = jnp.full((128, width), lens[e], jnp.int32)

        def half(n, first, second):
            token = lax.broadcasted_iota(jnp.int32, (128, width), 0) + (me * 256 + n * 128)
            weight = jnp.where(token < length, 1.0 / length.astype(F32), 0.0)
            total = own[e, n * 128 : n * 128 + 128, column:to] + (
                fin_in[e, first, :, column:to].astype(F32) + fin_in[e, second, :, column:to].astype(F32)
            )
            gath[e, me, n * 128 : n * 128 + 128, column:to] = (total * weight).astype(BF16)

        for n in (2, 5):
            rs_copy(i, n).wait_recv()
        half(0, 0, 2)
        if i not in STRAIGHT:
            ag_copy(i, 0).start()
        for n in (3, 4):
            rs_copy(i, n).wait_recv()
        half(1, 3, 1)
        if i in STRAIGHT:
            for z in (2, 1, 3):
                straight_copy(i, z).start()
        else:
            for n in (1, 2, 3):
                ag_copy(i, n).start()

    def forward(i):
        if i not in STRAIGHT:
            ag_copy(i, 0).wait_recv()
            ag_copy(i, 4).start()
            ag_copy(i, 1).wait_recv()
            ag_copy(i, 5).start()

    def a2a_columns(i):
        e, column, width = UNITS[i]
        return e, pl.ds(256 - column - width, width)

    def gradient(i):
        e, column, width = UNITS[i]
        if i in STRAIGHT:
            for z in (1, 3, 2):
                straight_copy(i, z).wait_recv()
        else:
            for n in (2, 3, 4, 5):
                ag_copy(i, n).wait_recv()
        for c in range(column, column + width, 128):
            buf = c_buf if c == 0 else a_buf
            other = gath[e, :, :, c : c + 128].reshape(1024, 128).T
            for w in range(4):
                wide = buf[e, :, :, w * 256 : w * 256 + 256].reshape(1024, 256)
                g = jnp.dot(other, wide, preferred_element_type=F32).T
                grads[e, w * 8 : w * 8 + 8, :, 128 - c : 256 - c] = g.astype(BF16).reshape(8, 32, 128)
        _, k = a2a_columns(i)
        pltpu.make_async_copy(grads.at[e, group, :, k], land.at[e, place, :, k], a2a_recv.at[i]).start()
        for x, y, c in PEERS:
            remote(
                grads.at[e, rank(x, y, c), :, k], land.at[e, place, :, k], a2a_send.at[i], a2a_recv.at[i],
                device(x, y, c),
            ).start()

    def arrive(i):
        e, k = a2a_columns(i)
        pltpu.make_async_copy(land.at[e, :, :, k], land.at[e, :, :, k], a2a_recv.at[i]).wait()
        turned[e % 2, :, :, k] = jnp.swapaxes(land[e, :, :, k].astype(F32), 0, 1).astype(BF16)

    def swap(e):
        return remote(
            contrib.at[e, 1 - core], cross.at[e], cross_send.at[e], cross_recv.at[e], device(0, 0, 1)
        )

    def blocks_ready(_):
        block_load.wait()

    def project(e):
        def half(h):
            def one(n, _):
                o = lax.div(n, 8) * 16 + h * 8 + lax.rem(n, 8)
                contrib[e, h, n] = jnp.dot(turned[e % 2, rows[o]], b_buf[o], preferred_element_type=F32)
                return 0

            lax.fori_loop(0, 32, one, 0, unroll=16)

        half(1 - core)
        swap(e).start()
        half(core)

    def scatter(e):
        swap(e).wait_recv()
        swapped[...] = jnp.swapaxes(contrib[e, core] + cross[e], 0, 1)
        summed[e] = swapped[...].astype(BF16).reshape(CHIPS, 2, 32, 128)
        for k, (x, y) in enumerate(SHIFTS):
            remote(
                summed.at[e, chip_at(x, y)], plane.at[e, k], plane_send.at[e], plane_recv.at[e], device(x, y, 0)
            ).start()
        for k in range(2):
            mine[e, k] = swapped[chip_at(0, 0) * 2 + k]

    def collect(e):
        pltpu.make_async_copy(plane.at[e], plane.at[e], plane_recv.at[e]).wait()
        total = mine[e]
        for k in range(len(SHIFTS)):
            total = total + plane[e, k].astype(F32)
        fsend[e] = total.reshape(2, 4, 8, 128)
        for c in (0, 1):
            for z in range(4):
                src, dst = fsend.at[e, cores[c], z_at[z]], frecv.at[e, core, me]
                if c == 0 and z == 0:
                    pltpu.make_async_copy(src, dst, fin_recv.at[e]).start()
                else:
                    remote(src, dst, fin_send.at[e], fin_recv.at[e], device(0, 0, c, z)).start()

    for copy in small:
        copy.wait()
    far_sums(0)
    near_sums(0)
    pl.semaphore_wait(barrier, len(others))

    order = (
        (low_far, 0), (low_near, 0), (low_far, 1), (low_near, 1), (relay, 0), (low_far, 2), (relay, 1),
        (finish, 0), (finish, 1), (forward, 0), (low_near, 2), (relay, 2), (forward, 1), (low_far, 3),
        (low_far, 4), (gradient, 0), (finish, 2), (low_near, 3), (relay, 3), (gradient, 1), (forward, 2),
        (low_near, 4), (relay, 4), (arrive, 0), (blocks_ready, 0), (project, 0), (low_far, 5), (scatter, 0),
        (finish, 3), (gradient, 2), (low_near, 5), (relay, 5), (arrive, 1), (project, 1), (finish, 4),
        (scatter, 1), (forward, 3), (gradient, 3), (arrive, 2), (forward, 4), (finish, 5), (forward, 5),
        (gradient, 4), (collect, 0), (collect, 1), (gradient, 5), (project, 2), (arrive, 3), (project, 3),
        (scatter, 2), (scatter, 3), (arrive, 4), (arrive, 5), (project, 4), (scatter, 4), (collect, 2),
        (collect, 3), (collect, 4),
    )
    for stage, n in order:
        stage(n)

    for e in range(SEQ):
        pltpu.make_async_copy(frecv.at[e], frecv.at[e], fin_recv.at[e]).wait()
        for h in range(2):
            out[e, h * 8 : h * 8 + 8] = (frecv[e, h, 0] + frecv[e, h, 1]) + (frecv[e, h, 2] + frecv[e, h, 3])

    for i in range(COUNT):
        for n in range(6):
            rs_copy(i, n).wait_send()
        if i in STRAIGHT:
            for z in (1, 2, 3):
                straight_copy(i, z).wait_send()
        else:
            for n in range(6):
                ag_copy(i, n).wait_send()
        e, k = a2a_columns(i)
        sent = land.at[e, pl.ds(0, 31), :, k]
        pltpu.make_async_copy(sent, sent, a2a_send.at[i]).wait()
    for e in range(SEQ):
        swap(e).wait_send()
        for ref, sem in (
            (plane.at[e], plane_send.at[e]),
            (fsend.at[e, 0, pl.ds(0, 3)], fin_send.at[e]),
            (fsend.at[e, 1], fin_send.at[e]),
        ):
            pltpu.make_async_copy(ref, ref, sem).wait()


def local(acts, cotangent, adapter_down, adapter_up, lengths, projection_rows, projection_blocks):
    vmem, hbm = (pl.BlockSpec(memory_space=m) for m in (pltpu.VMEM, pl.ANY))
    dma = pltpu.SemaphoreType.DMA
    out = pl.pallas_call(
        kernel,
        out_shape=jax.ShapeDtypeStruct((SEQ, 16, 128), F32),
        in_specs=[hbm] * 7,
        out_specs=vmem,
        scratch_shapes=[
            pltpu.VMEM((SEQ, 4, 256, 1024), BF16),
            pltpu.VMEM((SEQ, 4, 256, 1024), BF16),
            pltpu.VMEM((64, 256, 128), BF16),
            pltpu.VMEM((1024, 128), BF16),
            pltpu.VMEM((128, 1024), BF16),
            pltpu.SMEM((SEQ,), jnp.int32),
            pltpu.SMEM((64,), jnp.int32),
            pltpu.VMEM((SEQ, 256, 256), F32),
            pltpu.VMEM((SEQ, 2, 128, 256), F32),
            pltpu.VMEM((SEQ, 4, 2, 128, 256), BF16),
            pltpu.VMEM((SEQ, 2, 128, 256), BF16),
            pltpu.VMEM((SEQ, 4, 128, 256), BF16),
            pltpu.VMEM((SEQ, 4, 256, 256), BF16),
            pltpu.VMEM((SEQ, 32, 32, 256), BF16),
            pltpu.VMEM((SEQ, 32, 32, 256), BF16),
            pltpu.VMEM((2, 32, 32, 256), BF16),
            pltpu.VMEM((SEQ, 2, 32, 32, 128), F32),
            pltpu.VMEM((SEQ, 32, 32, 128), F32),
            pltpu.VMEM((32, 32, 128), F32),
            pltpu.VMEM((SEQ, CHIPS, 2, 32, 128), BF16),
            pltpu.VMEM((SEQ, 2, 32, 128), F32),
            pltpu.VMEM((SEQ, CHIPS - 1, 2, 32, 128), BF16),
            pltpu.VMEM((SEQ, 2, 4, 8, 128), F32),
            pltpu.VMEM((SEQ, 2, 4, 8, 128), F32),
            dma((2, SEQ)), dma((4,)), dma, dma((COUNT, 6)), dma((COUNT, 6)), dma((COUNT, 6)), dma((COUNT, 6)), dma((COUNT,)), dma((COUNT,)),
            dma((SEQ,)), dma((SEQ,)), dma((SEQ,)), dma((SEQ,)), dma((SEQ,)), dma((SEQ,)),
        ],
        compiler_params=pltpu.CompilerParams(
            collective_id=0, has_side_effects=True, vmem_limit_bytes=60 * 1024 * 1024
        ),
        cost_estimate=pl.CostEstimate(flops=6 * 10**9, bytes_accessed=25 * 10**6, transcendentals=0),
    )(
        acts.reshape(SEQ, 4, 256, 1024),
        cotangent.reshape(SEQ, 4, 256, 1024),
        adapter_down,
        adapter_up,
        lengths,
        projection_rows.reshape(64),
        projection_blocks.reshape(64, 256, 128),
    )
    return out.reshape(SEQ, 2048)


def solution(mesh):
    placed = (
        P(("dp", "proj"), None, "tensor"),
        P(("dp", "proj"), None, "tensor"),
        P("tensor", None),
        P(None, "tensor"),
        P(("dp", "proj")),
        P("tensor", ("dp", "proj"), None),
        P("tensor", ("dp", "proj"), None, None, None),
    )
    return jax.shard_map(
        local, mesh=mesh, in_specs=placed, out_specs=P(("dp", "proj"), "tensor"), check_vma=False
    )
```

time: 88.4 us -> 83.5 us (0.945)
  Pallas kernels: 86.8 us -> 81.9 us
    pallas_call x1, Pallas kernels: 86.8 us -> 81.9 us  [local(): pl.pallas_call(kernel, out_shape=jax.ShapeDtypeStruct((SEQ, 16, 128), F32...]
where the time goes in v4:
time: 83.5 us; the launch traced here: 83.4 us
  Pallas kernels  81.9 us (98%)
  local copies, waits for them, and re-layouts  1.43 us (2%)
    pallas_call x1, Pallas kernels, local(): pl.pallas_call(kernel, out_shape=jax.ShapeDtypeStruct((SEQ, 16, 128), F32...  81.9 us

profile of v4, /device:TPU:1, one launch (start us, length us, event | category | flops | bytes accessed | tf_op | source)
XLA Modules:
  0.0 83.4 jit_solution(15971347717211987577)
XLA Ops:
  0.0 81.9 %shard_map.73 = f32[5,16,128]{2,1,0:T(8,128)} custom-call(bf16[5,4,256,1024]{3,2,1,0:T(8,128)(2,1)} %bitcast.8, bf16[5,4,256,1024]{3,2,1,0:T(8,128)(2,1)} %bitcast.9, bf16[1024,128]{1,0:T(8,128)(2,1)} %down_in.1, bf16[128,1024]{1,0:T(8,128)(2,1)} %up_in.1, s32[5]{0:T(128)} %lens_in.1, s32[64]{0:T(128)} %bitcast.12, bf16[64,256,128]{2,1,0:T(8,128)(2,1)} %bitcast.10), custom_call_target="tpu_custom_call" | custom-call | flops 6000000000 | bytes 25000000 | tf_op jit(solution)/shard_map/pallas_call | solution.py:331
  82.0 1.4 %copy.10 = f32[1,5,16,128]{3,1,2,0:T(8,128)} copy(f32[1,5,16,128]{3,2,1,0:T(8,128)} %bitcast.11) | data formatting | bytes 81920

commit v5 on v4

--- a/solution.py
+++ b/solution.py
@@ -11,9 +11,10 @@
 F32 = jnp.float32
 BF16 = jnp.bfloat16
 SEQ = 5
-UNITS = ((0, 0, 256), (1, 0, 256), (2, 0, 256), (3, 0, 256), (4, 0, 128), (4, 128, 128))
+UNITS = ((0, 0, 128), (0, 128, 128), (1, 0, 256), (2, 0, 256), (3, 0, 256), (4, 0, 128), (4, 128, 128))
 COUNT = len(UNITS)
-STRAIGHT = (COUNT - 1,)
+PARTS = ((0, 0, 32), (1, 0, 32), (2, 0, 32), (3, 0, 32), (4, 0, 16), (4, 16, 16))
+STRAIGHT = ()
 CHIPS = 16
 
 
@@ -138,13 +139,13 @@
             relay_f[e, 1, :, c : c + 128] = value[0:128]
 
     def low_far(i):
-        if i:
+        if i > 1:
             far_sums(i)
         rs_copy(i, 0).start()
         rs_copy(i, 1).start()
 
     def low_near(i):
-        if i:
+        if i > 1:
             near_sums(i)
         rs_copy(i, 2).start()
         rs_copy(i, 3).start()
@@ -232,40 +233,55 @@
         pltpu.make_async_copy(land.at[e, :, :, k], land.at[e, :, :, k], a2a_recv.at[i]).wait()
         turned[e % 2, :, :, k] = jnp.swapaxes(land[e, :, :, k].astype(F32), 0, 1).astype(BF16)
 
-    def swap(e):
+    def swap(p):
+        e, first, count = PARTS[p]
+        blocks_of = pl.ds(first, count)
         return remote(
-            contrib.at[e, 1 - core], cross.at[e], cross_send.at[e], cross_recv.at[e], device(0, 0, 1)
+            contrib.at[e, 1 - core, blocks_of], cross.at[e, blocks_of], cross_send.at[p], cross_recv.at[p],
+            device(0, 0, 1),
         )
 
     def blocks_ready(_):
         block_load.wait()
 
-    def project(e):
+    def project(p):
+        e, first, count = PARTS[p]
+
         def half(h):
             def one(n, _):
                 o = lax.div(n, 8) * 16 + h * 8 + lax.rem(n, 8)
                 contrib[e, h, n] = jnp.dot(turned[e % 2, rows[o]], b_buf[o], preferred_element_type=F32)
                 return 0
 
-            lax.fori_loop(0, 32, one, 0, unroll=16)
+            lax.fori_loop(first, first + count, one, 0, unroll=16)
 
         half(1 - core)
-        swap(e).start()
+        swap(p).start()
         half(core)
 
-    def scatter(e):
-        swap(e).wait_recv()
-        swapped[...] = jnp.swapaxes(contrib[e, core] + cross[e], 0, 1)
-        summed[e] = swapped[...].astype(BF16).reshape(CHIPS, 2, 32, 128)
+    def plane_part(ref, p):
+        e, first, count = PARTS[p]
+        return ref.at[e, :, :, pl.ds(first, count)]
+
+    def scatter(p):
+        e, first, count = PARTS[p]
+        last = first + count
+        swap(p).wait_recv()
+        swapped[:, first:last] = jnp.swapaxes(contrib[e, core, first:last] + cross[e, first:last], 0, 1)
+        summed[e, :, :, first:last] = swapped[:, first:last].astype(BF16).reshape(CHIPS, 2, count, 128)
         for k, (x, y) in enumerate(SHIFTS):
             remote(
-                summed.at[e, chip_at(x, y)], plane.at[e, k], plane_send.at[e], plane_recv.at[e], device(x, y, 0)
+                summed.at[e, chip_at(x, y), :, pl.ds(first, count)], plane.at[e, k, :, pl.ds(first, count)],
+                plane_send.at[p], plane_recv.at[p], device(x, y, 0),
             ).start()
         for k in range(2):
-            mine[e, k] = swapped[chip_at(0, 0) * 2 + k]
+            mine[e, k, first:last] = swapped[chip_at(0, 0) * 2 + k, first:last]
 
     def collect(e):
-        pltpu.make_async_copy(plane.at[e], plane.at[e], plane_recv.at[e]).wait()
+        for p, (e_of, _, _) in enumerate(PARTS):
+            if e_of == e:
+                arrived = plane_part(plane, p)
+                pltpu.make_async_copy(arrived, arrived, plane_recv.at[p]).wait()
         total = mine[e]
         for k in range(len(SHIFTS)):
             total = total + plane[e, k].astype(F32)
@@ -280,20 +296,22 @@
 
     for copy in small:
         copy.wait()
-    far_sums(0)
-    near_sums(0)
+    for i in (0, 1):
+        far_sums(i)
+        near_sums(i)
     pl.semaphore_wait(barrier, len(others))
 
     order = (
-        (low_far, 0), (low_near, 0), (low_far, 1), (low_near, 1), (relay, 0), (low_far, 2), (relay, 1),
-        (finish, 0), (finish, 1), (forward, 0), (low_near, 2), (relay, 2), (forward, 1), (low_far, 3),
-        (low_far, 4), (gradient, 0), (finish, 2), (low_near, 3), (relay, 3), (gradient, 1), (forward, 2),
-        (low_near, 4), (relay, 4), (arrive, 0), (blocks_ready, 0), (project, 0), (low_far, 5), (scatter, 0),
-        (finish, 3), (gradient, 2), (low_near, 5), (relay, 5), (arrive, 1), (project, 1), (finish, 4),
-        (scatter, 1), (forward, 3), (gradient, 3), (arrive, 2), (forward, 4), (finish, 5), (forward, 5),
-        (gradient, 4), (collect, 0), (collect, 1), (gradient, 5), (project, 2), (arrive, 3), (project, 3),
-        (scatter, 2), (scatter, 3), (arrive, 4), (arrive, 5), (project, 4), (scatter, 4), (collect, 2),
-        (collect, 3), (collect, 4),
+        (low_far, 0), (low_far, 1), (low_far, 2), (low_near, 0), (low_near, 1), (relay, 0), (relay, 1),
+        (low_near, 2), (relay, 2), (finish, 0), (finish, 1), (low_far, 3), (forward, 0), (finish, 2),
+        (forward, 1), (low_near, 3), (relay, 3), (gradient, 0), (forward, 2), (gradient, 1), (low_far, 4),
+        (finish, 3), (gradient, 2), (low_near, 4), (relay, 4), (arrive, 0), (forward, 3), (low_far, 5),
+        (low_far, 6), (arrive, 1), (blocks_ready, 0), (project, 0), (low_near, 5), (scatter, 0), (finish, 4),
+        (gradient, 3), (low_near, 6), (arrive, 2), (relay, 5), (forward, 4), (relay, 6), (project, 1),
+        (scatter, 1), (finish, 5), (gradient, 4), (collect, 0), (finish, 6), (arrive, 3), (forward, 5),
+        (project, 2), (forward, 6), (gradient, 5), (gradient, 6), (arrive, 4), (project, 3), (scatter, 2),
+        (scatter, 3), (arrive, 5), (collect, 1), (arrive, 6), (project, 4), (project, 5), (scatter, 4),
+        (scatter, 5), (collect, 2), (collect, 3), (collect, 4),
     )
     for stage, n in order:
         stage(n)
@@ -301,7 +319,10 @@
     for e in range(SEQ):
         pltpu.make_async_copy(frecv.at[e], frecv.at[e], fin_recv.at[e]).wait()
         for h in range(2):
-            out[e, h * 8 : h * 8 + 8] = (frecv[e, h, 0] + frecv[e, h, 1]) + (frecv[e, h, 2] + frecv[e, h, 3])
+            total = (frecv[e, h, 0] + frecv[e, h, 1]) + (frecv[e, h, 2] + frecv[e, h, 3])
+            for n in range(8):
+                o = h * 8 + n
+                out[e : e + 1, o * 128 : o * 128 + 128] = total[n : n + 1]
 
     for i in range(COUNT):
         for n in range(6):
@@ -315,10 +336,12 @@
         e, k = a2a_columns(i)
         sent = land.at[e, pl.ds(0, 31), :, k]
         pltpu.make_async_copy(sent, sent, a2a_send.at[i]).wait()
+    for p in range(len(PARTS)):
+        swap(p).wait_send()
+        sent = plane_part(plane, p)
+        pltpu.make_async_copy(sent, sent, plane_send.at[p]).wait()
     for e in range(SEQ):
-        swap(e).wait_send()
         for ref, sem in (
-            (plane.at[e], plane_send.at[e]),
             (fsend.at[e, 0, pl.ds(0, 3)], fin_send.at[e]),
             (fsend.at[e, 1], fin_send.at[e]),
         ):
@@ -328,9 +351,9 @@
 def local(acts, cotangent, adapter_down, adapter_up, lengths, projection_rows, projection_blocks):
     vmem, hbm = (pl.BlockSpec(memory_space=m) for m in (pltpu.VMEM, pl.ANY))
     dma = pltpu.SemaphoreType.DMA
-    out = pl.pallas_call(
+    return pl.pallas_call(
         kernel,
-        out_shape=jax.ShapeDtypeStruct((SEQ, 16, 128), F32),
+        out_shape=jax.ShapeDtypeStruct((SEQ, 2048), F32),
         in_specs=[hbm] * 7,
         out_specs=vmem,
         scratch_shapes=[
@@ -359,7 +382,7 @@
             pltpu.VMEM((SEQ, 2, 4, 8, 128), F32),
             pltpu.VMEM((SEQ, 2, 4, 8, 128), F32),
             dma((2, SEQ)), dma((4,)), dma, dma((COUNT, 6)), dma((COUNT, 6)), dma((COUNT, 6)), dma((COUNT, 6)), dma((COUNT,)), dma((COUNT,)),
-            dma((SEQ,)), dma((SEQ,)), dma((SEQ,)), dma((SEQ,)), dma((SEQ,)), dma((SEQ,)),
+            dma((len(PARTS),)), dma((len(PARTS),)), dma((len(PARTS),)), dma((len(PARTS),)), dma((SEQ,)), dma((SEQ,)),
         ],
         compiler_params=pltpu.CompilerParams(
             collective_id=0, has_side_effects=True, vmem_limit_bytes=60 * 1024 * 1024
@@ -374,7 +397,6 @@
         projection_rows.reshape(64),
         projection_blocks.reshape(64, 256, 128),
     )
-    return out.reshape(SEQ, 2048)
 
 
 def solution(mesh):

time: 83.5 us -> 81.9 us (0.981)
  Pallas kernels: 81.9 us -> 80.2 us
    pallas_call x1, Pallas kernels: 81.9 us -> 80.2 us  [local(): pl.pallas_call(kernel, out_shape=jax.ShapeDtypeStruct((SEQ, 2048), F32),...]
where the time goes in v5:
time: 81.9 us; the launch traced here: 81.7 us
  Pallas kernels  80.2 us (98%)
  local copies, waits for them, and re-layouts  1.47 us (2%)
    pallas_call x1, Pallas kernels, local(): pl.pallas_call(kernel, out_shape=jax.ShapeDtypeStruct((SEQ, 2048), F32),...  80.2 us

profile of v5, /device:TPU:1, one launch (start us, length us, event | category | flops | bytes accessed | tf_op | source)
XLA Modules:
  0.0 81.7 jit_solution(12954783603088803400)
XLA Ops:
  0.0 80.2 %shard_map.73 = f32[5,2048]{1,0:T(8,128)} custom-call(bf16[5,4,256,1024]{3,2,1,0:T(8,128)(2,1)} %bitcast.4, bf16[5,4,256,1024]{3,2,1,0:T(8,128)(2,1)} %bitcast.5, bf16[1024,128]{1,0:T(8,128)(2,1)} %down_in.1, bf16[128,1024]{1,0:T(8,128)(2,1)} %up_in.1, s32[5]{0:T(128)} %lens_in.1, s32[64]{0:T(128)} %bitcast.7, bf16[64,256,128]{2,1,0:T(8,128)(2,1)} %bitcast.6), custom_call_target="tpu_custom_call" | custom-call | flops 6000000000 | bytes 25000000 | tf_op jit(solution)/shard_map/pallas_call | solution.py:354
  80.2 1.5 %copy.9 = f32[5,2048]{1,0:T(8,128)} copy(f32[5,2048]{1,0:T(8,128)} %shard_map.73) | data formatting | bytes 81920

commit v6 on v5

--- a/solution.py
+++ b/solution.py
@@ -139,13 +139,13 @@
             relay_f[e, 1, :, c : c + 128] = value[0:128]
 
     def low_far(i):
-        if i > 1:
+        if i:
             far_sums(i)
         rs_copy(i, 0).start()
         rs_copy(i, 1).start()
 
     def low_near(i):
-        if i > 1:
+        if i:
             near_sums(i)
         rs_copy(i, 2).start()
         rs_copy(i, 3).start()
@@ -296,9 +296,8 @@
 
     for copy in small:
         copy.wait()
-    for i in (0, 1):
-        far_sums(i)
-        near_sums(i)
+    far_sums(0)
+    near_sums(0)
     pl.semaphore_wait(barrier, len(others))
 
     order = (

time: 81.9 us -> 81.6 us (level)
  no operation moved by 1% of the time
where the time goes in v6:
time: 81.6 us; the launch traced here: 81.5 us
  Pallas kernels  80 us (98%)
  local copies, waits for them, and re-layouts  1.47 us (2%)
    pallas_call x1, Pallas kernels, local(): pl.pallas_call(kernel, out_shape=jax.ShapeDtypeStruct((SEQ, 2048), F32),...  80 us

profile of v6, /device:TPU:1, one launch (start us, length us, event | category | flops | bytes accessed | tf_op | source)
XLA Modules:
  0.0 81.5 jit_solution(13672250262986559927)
XLA Ops:
  0.0 80.0 %shard_map.73 = f32[5,2048]{1,0:T(8,128)} custom-call(bf16[5,4,256,1024]{3,2,1,0:T(8,128)(2,1)} %bitcast.4, bf16[5,4,256,1024]{3,2,1,0:T(8,128)(2,1)} %bitcast.5, bf16[1024,128]{1,0:T(8,128)(2,1)} %down_in.1, bf16[128,1024]{1,0:T(8,128)(2,1)} %up_in.1, s32[5]{0:T(128)} %lens_in.1, s32[64]{0:T(128)} %bitcast.7, bf16[64,256,128]{2,1,0:T(8,128)(2,1)} %bitcast.6), custom_call_target="tpu_custom_call" | custom-call | flops 6000000000 | bytes 25000000 | tf_op jit(solution)/shard_map/pallas_call | solution.py:353
  80.0 1.5 %copy.9 = f32[5,2048]{1,0:T(8,128)} copy(f32[5,2048]{1,0:T(8,128)} %shard_map.73) | data formatting | bytes 81920
